TPU v7x, 32 devices: a whole 2x2x4 slice. The times are simulated.
32 devices in a mesh: groups: 2 (over x), owners: 16 (over z, y, core).
Axes of the slice: x: 2, y: 2, z: 4, core: 2. Of those that a mesh axis runs over, the one named last changes fastest.
Arguments:
- embeddings: float32 [8192, 768], P(('groups', 'owners')), parts along dimension 0, may hold values from -6 to 6
- cluster_ids: int32 [8192], P(('groups', 'owners')), parts along dimension 0, may hold values from 0 to 255, as said below
Outputs:
- best_match: float32 [8192], P(('groups', 'owners')), parts along dimension 0
There are 2 independent parts, one for each index of `groups`. A program takes and returns all parts, laid end to end along the dimension named above; each array names one. Nothing has to cross between parts.
Inputs may be any that keep to these rules, and one draw needn't show every extreme that they name: `cluster_ids`: cluster c is owned by device c mod (16) of the owners axis. The rows of one data shard (aligned blocks of 256 rows) fall in clusters of either none or exactly 32 rows for each owner.
All inputs are finite; a program needn't handle non-finite values.
Results may differ from a plain program's by a relative error of at most 0.0001.
Values sent between devices are 32-bit elements; how exact they have to be, the bound alone decides.
A program may use at most 64 MiB of HBM per device.

v0:
```python
import math

import jax
import jax.numpy as jnp
from jax import lax
from jax.sharding import PartitionSpec as P


def to_unit(rows):
    return rows / jnp.sqrt(jnp.sum(rows * rows, axis=-1, keepdims=True) + 1e-06)


def shards(embeddings, cluster_ids):
    rows, width = embeddings.shape
    owners = lax.axis_size("owners")
    me = lax.axis_index("owners")
    capacity = max(rows * 2 // owners, 2)
    total = owners * capacity
    dest = cluster_ids % owners
    positions = jnp.arange(rows, dtype=jnp.int32)
    same_dest = (dest[:, None] == dest[None, :]) & (positions[None, :] < positions[:, None])
    rank = jnp.sum(same_dest.astype(jnp.int32), axis=1)
    slot_of_row = dest * capacity + rank
    placing = (jnp.arange(total, dtype=jnp.int32)[:, None] == slot_of_row[None, :]).astype(
        jnp.float32
    )
    global_idx = (me * rows + positions).astype(jnp.float32)
    payload = to_unit(embeddings)
    send_rows = jnp.dot(
        placing, payload, precision=lax.Precision.HIGHEST, preferred_element_type=jnp.float32
    ).reshape(owners, capacity, width)
    labels = jnp.stack([global_idx + 1.0, cluster_ids.astype(jnp.float32) + 1.0], axis=1)
    placed_labels = (
        jnp.dot(
            placing, labels, precision=lax.Precision.HIGHEST, preferred_element_type=jnp.float32
        )
        - 1.0
    )
    send_idx = placed_labels[:, 0].reshape(owners, capacity)
    send_clu = placed_labels[:, 1].reshape(owners, capacity)
    got_rows, got_idx, got_clu = (
        lax.all_to_all(send_rows, "owners", split_axis=0, concat_axis=0, tiled=True),
        lax.all_to_all(send_idx, "owners", split_axis=0, concat_axis=0, tiled=True),
        lax.all_to_all(send_clu, "owners", split_axis=0, concat_axis=0, tiled=True),
    )
    flat_rows = got_rows.reshape(total, width)
    flat_idx = got_idx.reshape(total)
    flat_clu = got_clu.reshape(total)
    block = math.gcd(total, 512)

    def one_block(inputs):
        query, query_idx, query_clu = inputs
        scores = jnp.dot(
            query, flat_rows.T, precision=lax.Precision.HIGHEST, preferred_element_type=jnp.float32
        )
        valid = (
            (flat_idx[None, :] >= 0.0)
            & (flat_clu[None, :] == query_clu[:, None])
            & (flat_idx[None, :] < query_idx[:, None])
        )
        return jnp.max(jnp.where(valid, scores, jnp.float32(-1.0)), axis=1)

    best = lax.map(
        one_block,
        (
            flat_rows.reshape(total // block, block, width),
            flat_idx.reshape(total // block, block),
            flat_clu.reshape(total // block, block),
        ),
    )
    back = lax.all_to_all(
        best.reshape(owners, capacity), "owners", split_axis=0, concat_axis=0, tiled=True
    )
    return jnp.dot(
        back.reshape(1, total),
        placing,
        precision=lax.Precision.HIGHEST,
        preferred_element_type=jnp.float32,
    ).reshape(rows)


def solution(mesh):
    in_specs = (P(("groups", "owners"), None), P(("groups", "owners")))
    out_specs = P(("groups", "owners"))
    return jax.shard_map(shards, mesh=mesh, in_specs=in_specs, out_specs=out_specs, check_vma=False)
```

profile of v0, /device:TPU:0, one launch (start us, length us, event | category | flops | bytes accessed | tf_op | source)
XLA Modules:
  0.0 82.3 jit_solution(3351038387649950923)
XLA Ops:
  0.0 0.7 and_select_fusion
  0.7 0.7 convert_add_fusion
  1.4 0.2 convert_reduce_fusion
  1.5 0.7 multiply_add_fusion
  2.3 0.3 convolution_add_fusion
  2.6 0.1 slice_reduce_fusion
  2.6 0.7 all_to_all.21
  3.3 7.4 %all-to-all-start = ((f32[16,1,32]{2,1,0:T(1,128)}), f32[16,1,32]{2,1,0:T(1,128)S(1)}, u32[]{:S(2)}, u32[]{:S(2)}) async-start(f32[16,1,32]{2,1,0:T(1,128)} %bitcast.1), calls=%async_computation | async-start | bytes 16384 | tf_op jit(solution)/shard_map/all_to_all | solution.py:43
  10.7 1.3 %multiply_reduce_fusion = f32[256]{0:T(256)S(1)} fusion(f32[256,768]{1,0:T(8,128)} %param.2), kind=kLoop, calls=%fused_computation.5 | loop fusion | flops 392960 | bytes 787456 | tf_op jit(solution)/shard_map/reduce_sum | solution.py:10
  12.0 0.7 all_to_all.23
  12.6 4.5 %all-to-all-done = f32[16,1,32]{2,1,0:T(1,128)S(1)} async-done(((f32[16,1,32]{2,1,0:T(1,128)}), f32[16,1,32]{2,1,0:T(1,128)S(1)}, u32[]{:S(2)}, u32[]{:S(2)}) %all-to-all-start) | async-done | bytes 2080 | tf_op jit(solution)/shard_map/all_to_all | solution.py:43
  17.1 3.4 %all-to-all-start.1 = ((f32[16,1,32]{2,1,0:T(1,128)}), f32[16,1,32]{2,1,0:T(1,128)S(1)}, u32[]{:S(2)}, u32[]{:S(2)}) async-start(f32[16,1,32]{2,1,0:T(1,128)} %bitcast.2), calls=%async_computation.1 | async-start | bytes 16384 | tf_op jit(solution)/shard_map/all_to_all | solution.py:44
  20.6 3.3 %fusion.1 = f32[512,768]{1,0:T(8,128)} fusion(f32[256,768]{1,0:T(8,128)} %param.2, f32[256]{0:T(256)S(1)} %add_sqrt_fusion, s32[256]{0:T(256)S(1)} %multiply_add_fusion), kind=kOutput, calls=%fused_computation.3 | convolution fusion | flops 1208287232 | bytes 2361344 | tf_op jit(solution)/shard_map/dot_general | solution.py:29
  23.8 3.1 %all-to-all-done.1 = f32[16,1,32]{2,1,0:T(1,128)S(1)} async-done(((f32[16,1,32]{2,1,0:T(1,128)}), f32[16,1,32]{2,1,0:T(1,128)S(1)}, u32[]{:S(2)}, u32[]{:S(2)}) %all-to-all-start.1) | async-done | bytes 2080 | tf_op jit(solution)/shard_map/all_to_all | solution.py:44
  26.9 3.7 %all-to-all-start.2 = ((f32[16,32,768]{2,1,0:T(8,128)}), f32[16,32,768]{2,1,0:T(8,128)S(1)}, u32[]{:S(2)}, u32[]{:S(2)}) async-start(f32[16,32,768]{2,1,0:T(8,128)} %bitcast.3), calls=%async_computation.2 | async-start | bytes 3145728 | tf_op jit(solution)/shard_map/all_to_all | solution.py:42
  30.6 0.5 broadcast.71
  31.1 0.7 reduce.17
  31.8 0.1 broadcast_in_dim_reshape.7
  31.9 0.7 reduce.18
  32.6 0.1 eq.56
  32.7 29.9 %all-to-all-done.2 = f32[16,32,768]{2,1,0:T(8,128)S(1)} async-done(((f32[16,32,768]{2,1,0:T(8,128)}), f32[16,32,768]{2,1,0:T(8,128)S(1)}, u32[]{:S(2)}, u32[]{:S(2)}) %all-to-all-start.2) | async-done | bytes 1572896 | tf_op jit(solution)/shard_map/all_to_all | solution.py:42
  62.5 2.8 %fusion = f32[512]{0:T(512)S(1)} fusion(f32[512,768]{1,0:T(8,128)S(1)} %bitcast.9, f32[512]{0:T(512)S(1)} %broadcast_in_dim_reshape.7, f32[512]{0:T(512)S(1)} %eq.56, pred[512]{0:T(512)(128)(4,1)S(1)} %broadcast_compare_fusion), kind=kOutput, calls=%fused_computation.1 | convolution fusion | flops 2417491456 | bytes 1579520 | tf_op jit(solution)/shard_map/while/body/eval_jaxpr/dot_general | solution.py:53
  65.4 0.1 all_to_all.26
  65.4 15.3 %all_to_all.32 = f32[16,1,32]{2,1,0:T(1,128)S(1)} all-to-all(f32[16,1,32]{2,1,0:T(1,128)S(1)} %all_to_all.26), channel_id=1, replica_groups=mesh['groups'=2,'owners'=16] {'owners'}, dimensions={0} | all-to-all | bytes 4096 | tf_op jit(solution)/shard_map/all_to_all | solution.py:71
  80.7 0.7 reduce.19
  81.4 0.1 reshape.69
  81.5 0.8 %fusion.3 = f32[1,256]{1,0:T(1,128)} fusion(f32[512,1]{0,1:T(1,128)S(1)} %reshape.69, s32[256]{0:T(256)S(1)} %multiply_add_fusion), kind=kOutput, calls=%fused_computation.7 | convolution fusion | flops 1703936 | bytes 4096 | tf_op jit(solution)/shard_map/dot_general | solution.py:74
  (3 shorter events, 0.0 us)
Async XLA Ops:
  3.3 13.8 %all-to-all-start = ((f32[16,1,32]{2,1,0:T(1,128)}), f32[16,1,32]{2,1,0:T(1,128)S(1)}, u32[]{:S(2)}, u32[]{:S(2)}) async-start(f32[16,1,32]{2,1,0:T(1,128)} %bitcast.1), calls=%async_computation | async-start | bytes 16384 | tf_op jit(solution)/shard_map/all_to_all | solution.py:43
  17.1 9.8 %all-to-all-start.1 = ((f32[16,1,32]{2,1,0:T(1,128)}), f32[16,1,32]{2,1,0:T(1,128)S(1)}, u32[]{:S(2)}, u32[]{:S(2)}) async-start(f32[16,1,32]{2,1,0:T(1,128)} %bitcast.2), calls=%async_computation.1 | async-start | bytes 16384 | tf_op jit(solution)/shard_map/all_to_all | solution.py:44
  26.9 35.6 %all-to-all-start.2 = ((f32[16,32,768]{2,1,0:T(8,128)}), f32[16,32,768]{2,1,0:T(8,128)S(1)}, u32[]{:S(2)}, u32[]{:S(2)}) async-start(f32[16,32,768]{2,1,0:T(8,128)} %bitcast.3), calls=%async_computation.2 | async-start | bytes 3145728 | tf_op jit(solution)/shard_map/all_to_all | solution.py:42
where the time goes:
time: 82.8 us; the launch traced here: 82.3 us
  waiting for transfers between devices  37.4 us (45%)
  blocking collectives  15.3 us (18%)
  starting transfers between devices  14.5 us (18%)
  matrix products  7.25 us (9%)
  other arithmetic  5.54 us (7%)
  local copies, waits for them, and re-layouts  2.24 us (3%)
    all_to_all x1, waiting for transfers between devices, shards(): lax.all_to_all(send_rows, 'owners', split_axis=0, concat_axis=0, tiled=True)  29.9 us
    all_to_all x1, blocking collectives, shards(): lax.all_to_all(best.reshape(owners, capacity), 'owners', split_axis=0, co...  15.3 us
    all_to_all x1, starting transfers between devices, shards(): lax.all_to_all(send_idx, 'owners', split_axis=0, concat_axis=0, tiled=True)  7.39 us
    all_to_all x1, waiting for transfers between devices, shards(): lax.all_to_all(send_idx, 'owners', split_axis=0, concat_axis=0, tiled=True)  4.45 us
    all_to_all x1, starting transfers between devices, shards(): lax.all_to_all(send_rows, 'owners', split_axis=0, concat_axis=0, tiled=True)  3.71 us
    all_to_all x1, starting transfers between devices, shards(): lax.all_to_all(send_clu, 'owners', split_axis=0, concat_axis=0, tiled=True)  3.45 us
    dot_general x1, matrix products, shards(): jnp.dot(placing, payload, precision=lax.Precision.HIGHEST, preferred_elem...  3.29 us
    all_to_all x1, waiting for transfers between devices, shards(): lax.all_to_all(send_clu, 'owners', split_axis=0, concat_axis=0, tiled=True)  3.07 us
  transfers between devices with their start and end apart: 3, of which 3 were waited for; matrix products, arithmetic and copies ran while one was open for 8% of the time, Pallas kernels for 0%

commit v1 on v0

--- a/solution.py
+++ b/solution.py
@@ -1,16 +1,242 @@
+import functools
 import math
 
 import jax
 import jax.numpy as jnp
 from jax import lax
+from jax.experimental import pallas as pl
+from jax.experimental.pallas import tpu as pltpu
 from jax.sharding import PartitionSpec as P
+
+LANES = 128
+MESH = pl.DeviceIdType.MESH
+NT = (((1,), (1,)), ((), ()))
+ORDER = (2, 3, 1, 0)
 
 
 def to_unit(rows):
     return rows / jnp.sqrt(jnp.sum(rows * rows, axis=-1, keepdims=True) + 1e-06)
 
 
-def shards(embeddings, cluster_ids):
+def split(x):
+    high = x.astype(jnp.bfloat16)
+    low = (x - high.astype(jnp.float32)).astype(jnp.bfloat16)
+    return high, low
+
+
+def dedup_kernel(
+    n, cap, emb_ref, clu_ref, out_ref,
+    unit_hi, unit_lo, slot_of, send_rows, got_rows, got_hi, got_lo,
+    send_lab, got_lab, lab_col, best, got_best,
+    row_send, row_recv, lab_send, lab_recv, best_send, best_recv,
+):
+    rows, width = emb_ref.shape
+    per = LANES // cap
+    planes = n // per
+    me = lax.axis_index("owners")
+    my_plane = me // per
+
+    def plane_at(step):
+        if planes == 4:
+            return lax.bitwise_xor(my_plane, jnp.int32(step))
+        return lax.rem(my_plane + step, planes)
+
+    barrier = pltpu.get_barrier_semaphore()
+
+    def greet(step, _):
+        peer = lax.rem(me + step, n)
+        pl.semaphore_signal(barrier, inc=1, device_id={"owners": peer}, device_id_type=MESH)
+        return 0
+
+    lax.fori_loop(1, n, greet, 0)
+
+    clu = clu_ref[...].astype(jnp.float32)
+    label = jnp.floor((clu + 0.5) * (1.0 / n))
+    dest = clu - label * n
+    label = label + 1.0
+    owner = lax.broadcasted_iota(jnp.int32, (n, rows), 0).astype(jnp.float32)
+    mine = dest == owner
+    member = mine.astype(jnp.bfloat16)
+    earlier = (
+        lax.broadcasted_iota(jnp.int32, (rows, rows), 0)
+        < lax.broadcasted_iota(jnp.int32, (rows, rows), 1)
+    ).astype(jnp.bfloat16)
+    ranks = jnp.dot(member, earlier, preferred_element_type=jnp.float32)
+    slot_of[...] = jnp.where(mine, ranks, -1.0)
+    rank = jnp.sum(jnp.where(mine, ranks, 0.0), axis=0, keepdims=True)
+
+    lane_of = lax.broadcasted_iota(jnp.int32, (LANES, rows), 0).astype(jnp.float32)
+    placed_labels = lax.dot_general(
+        jnp.where(mine, label, 0.0), (lane_of == rank).astype(jnp.float32), NT,
+        precision=lax.Precision.HIGHEST, preferred_element_type=jnp.float32,
+    )
+    for o in range(n):
+        send_lab[o] = placed_labels[o : o + 1]
+
+    unit = to_unit(emb_ref[...])
+    unit_hi[...], unit_lo[...] = split(unit)
+
+    pl.semaphore_wait(barrier, n - 1)
+
+    def label_copy(peer):
+        return pltpu.make_async_remote_copy(
+            src_ref=send_lab.at[peer], dst_ref=got_lab.at[me],
+            send_sem=lab_send.at[peer], recv_sem=lab_recv.at[me],
+            device_id={"owners": peer}, device_id_type=MESH,
+        )
+
+    def row_copy(peer):
+        return pltpu.make_async_remote_copy(
+            src_ref=send_rows.at[peer], dst_ref=got_rows.at[me],
+            send_sem=row_send.at[peer], recv_sem=row_recv.at[me],
+            device_id={"owners": peer}, device_id_type=MESH,
+        )
+
+    def best_copy(peer):
+        return pltpu.make_async_remote_copy(
+            src_ref=best.at[peer // per], dst_ref=got_best.at[me],
+            send_sem=best_send.at[peer], recv_sem=best_recv.at[me],
+            device_id={"owners": peer}, device_id_type=MESH,
+        )
+
+    def arrived(buffer, sems, source):
+        pltpu.make_async_remote_copy(
+            src_ref=buffer.at[source], dst_ref=buffer.at[source],
+            send_sem=sems.at[source], recv_sem=sems.at[source],
+            device_id={"owners": source}, device_id_type=MESH,
+        ).wait_recv()
+
+    def others(do):
+        def step_of(step, _):
+            do(lax.rem(me + step, n))
+            return 0
+
+        lax.fori_loop(1, n, step_of, 0)
+
+    got_lab[me] = send_lab[me]
+
+    place = lax.broadcasted_iota(jnp.int32, (cap, rows), 0).astype(jnp.float32)
+    order = ORDER if planes == 4 else tuple(range(planes))[::-1]
+    for number, step in enumerate(order):
+        first = plane_at(step) * per
+        placing = jnp.concatenate(
+            [(place == slot_of[pl.ds(first + i, 1), :]).astype(jnp.float32) for i in range(per)], axis=0
+        ).astype(jnp.bfloat16)
+        block = jnp.dot(placing, unit_hi[...], preferred_element_type=jnp.float32) + jnp.dot(
+            placing, unit_lo[...], preferred_element_type=jnp.float32
+        )
+        for i in range(per):
+            send_rows[first + i] = block[i * cap : (i + 1) * cap]
+        for i in range(per):
+            peer = first + i
+            if step == 0:
+                @pl.when(peer != me)
+                def _():
+                    row_copy(peer).start()
+            else:
+                row_copy(peer).start()
+        if number == 0:
+            others(lambda peer: label_copy(peer).start())
+
+    got_rows[me] = send_rows[me]
+
+    others(lambda peer: arrived(got_lab, lab_recv, peer))
+    eye = lax.broadcasted_iota(jnp.int32, (cap, LANES), 0) == lax.broadcasted_iota(
+        jnp.int32, (cap, LANES), 1
+    )
+    for plane in range(planes):
+        for i in range(per):
+            column = jnp.sum(
+                jnp.where(eye, got_lab[plane * per + i], 0.0), axis=1, keepdims=True
+            )
+            lab_col[plane, pl.ds(i * cap, cap), :] = jnp.broadcast_to(column, (cap, LANES))
+        best[plane] = jnp.full((1, LANES), -1.0, jnp.float32)
+
+    square = (LANES, LANES)
+    row_at = lax.broadcasted_iota(jnp.int32, square, 0)
+    lane_at = lax.broadcasted_iota(jnp.int32, square, 1)
+    for step in range(planes):
+        new = plane_at(step)
+        for i in range(per):
+            source = new * per + i
+            if step == 0:
+                @pl.when(source != me)
+                def _():
+                    arrived(got_rows, row_recv, source)
+            else:
+                arrived(got_rows, row_recv, source)
+        block = got_rows[pl.ds(new * per, per)].reshape(LANES, width)
+        got_hi[new], got_lo[new] = split(block)
+        for past in range(step + 1):
+            old = plane_at(past)
+            low, high = jnp.minimum(old, new), jnp.maximum(old, new)
+            scores = (
+                lax.dot_general(got_hi[low], got_hi[high], NT, preferred_element_type=jnp.float32)
+                + lax.dot_general(got_hi[low], got_lo[high], NT, preferred_element_type=jnp.float32)
+                + lax.dot_general(got_lo[low], got_hi[high], NT, preferred_element_type=jnp.float32)
+            )
+            candidate = lab_col[low]
+            query = lab_col[high].T
+            valid = (candidate == query) & (candidate > 0.0)
+            if past == step:
+                valid = valid & (row_at < lane_at)
+            top = jnp.max(jnp.where(valid, scores, -1.0), axis=0, keepdims=True)
+            best[high] = jnp.maximum(best[high], top)
+
+    got_best[me] = best[my_plane]
+    others(lambda peer: best_copy(peer).start())
+    others(lambda peer: arrived(got_best, best_recv, peer))
+
+    offset = (lax.rem(me, per) * cap).astype(jnp.float32)
+    back = jnp.concatenate([got_best[o] for o in range(n)], axis=0)
+    spread = jnp.dot(
+        back, (lane_of == rank + offset).astype(jnp.float32),
+        precision=lax.Precision.HIGHEST, preferred_element_type=jnp.float32,
+    )
+    out_ref[...] = jnp.sum(jnp.where(mine, spread, 0.0), axis=0, keepdims=True)
+
+    def drain(peer):
+        row_copy(peer).wait_send()
+        label_copy(peer).wait_send()
+        best_copy(peer).wait_send()
+
+    others(drain)
+
+
+def fused(embeddings, cluster_ids):
+    rows, width = embeddings.shape
+    n = lax.axis_size("owners")
+    cap = rows * 2 // n
+    planes = n * cap // LANES
+    f32, bf16, dma = jnp.float32, jnp.bfloat16, pltpu.SemaphoreType.DMA
+    out = pl.pallas_call(
+        functools.partial(dedup_kernel, n, cap),
+        out_shape=jax.ShapeDtypeStruct((1, rows), f32),
+        in_specs=[pl.BlockSpec(memory_space=pltpu.VMEM)] * 2,
+        out_specs=pl.BlockSpec(memory_space=pltpu.VMEM),
+        scratch_shapes=[
+            pltpu.VMEM((rows, width), bf16),
+            pltpu.VMEM((rows, width), bf16),
+            pltpu.VMEM((n, rows), f32),
+            pltpu.VMEM((n, cap, width), f32),
+            pltpu.VMEM((n, cap, width), f32),
+            pltpu.VMEM((planes, LANES, width), bf16),
+            pltpu.VMEM((planes, LANES, width), bf16),
+            pltpu.VMEM((n, 1, LANES), f32),
+            pltpu.VMEM((n, 1, LANES), f32),
+            pltpu.VMEM((planes, LANES, LANES), f32),
+            pltpu.VMEM((planes, 1, LANES), f32),
+            pltpu.VMEM((n, 1, LANES), f32),
+        ]
+        + [dma((n,))] * 6,
+        compiler_params=pltpu.CompilerParams(
+            collective_id=0, has_side_effects=True, vmem_limit_bytes=32 * 1024 * 1024
+        ),
+    )(embeddings, cluster_ids.reshape(1, rows))
+    return out.reshape(rows)
+
+
+def plain(embeddings, cluster_ids):
     rows, width = embeddings.shape
     owners = lax.axis_size("owners")
     me = lax.axis_index("owners")
@@ -79,6 +305,16 @@
     ).reshape(rows)
 
 
+def shards(embeddings, cluster_ids):
+    rows, width = embeddings.shape
+    n = lax.axis_size("owners")
+    cap = rows * 2 // n
+    fits = cap % 8 == 0 and LANES % cap == 0 and n % (LANES // cap) == 0
+    if fits and rows % LANES == 0 and width % LANES == 0:
+        return fused(embeddings, cluster_ids)
+    return plain(embeddings, cluster_ids)
+
+
 def solution(mesh):
     in_specs = (P(("groups", "owners"), None), P(("groups", "owners")))
     out_specs = P(("groups", "owners"))

time: 82.8 us -> 49.7 us (0.60)
  Pallas kernels: 0 us -> 47.2 us
  waiting for transfers between devices: 37.4 us -> 0 us
  blocking collectives: 15.3 us -> 0 us
  starting transfers between devices: 14.5 us -> 0 us
  matrix products: 7.25 us -> 0 us
  other arithmetic: 5.54 us -> 0 us
    pallas_call x0 -> x1, Pallas kernels: none -> 47.2 us  [fused(): pl.pallas_call(functools.partial(dedup_kernel, n, cap), out_shape=jax.Sha...]
    all_to_all x3 -> x0, waiting for transfers between devices: 37.4 us -> none  [the longest x1 29.9 us: shards(): lax.all_to_all(send_rows, 'owners', split_axis=0, concat_axis=0, tiled=True)]
    all_to_all x1 -> x0, blocking collectives: 15.3 us -> none  [shards(): lax.all_to_all(best.reshape(owners, capacity), 'owners', split_axis=0, co...]
    all_to_all x3 -> x0, starting transfers between devices: 14.5 us -> none  [the longest x1 7.39 us: shards(): lax.all_to_all(send_idx, 'owners', split_axis=0, concat_axis=0, tiled=True)]
    dot_general x4 -> x0, matrix products: 7.25 us -> none  [the longest x1 3.29 us: shards(): jnp.dot(placing, payload, precision=lax.Precision.HIGHEST, preferred_elem...]
    unnamed x0 -> x5, local copies, waits for them, and re-layouts: none -> 2.38 us
    all_to_all x3 -> x0, other arithmetic: 2.01 us -> none  [the longest x1 0.67 us: shards(): lax.all_to_all(send_clu, 'owners', split_axis=0, concat_axis=0, tiled=True)]
    all_to_all x4 -> x0, local copies, waits for them, and re-layouts: 1.95 us -> none  [the longest x2 1.19 us: shards(): lax.all_to_all(send_idx, 'owners', split_axis=0, concat_axis=0, tiled=True)]
  transfers between devices with their start and end apart: 3 -> 0, of which waited for: 3 -> 0; matrix products, arithmetic and copies ran while one was open for 8% -> 0% of each run, Pallas kernels for 0% -> 0%
where the time goes in v1:
time: 49.7 us; the launch traced here: 49.5 us
  Pallas kernels  47.2 us (95%)
  local copies, waits for them, and re-layouts  2.38 us (5%)
    pallas_call x1, Pallas kernels, fused(): pl.pallas_call(functools.partial(dedup_kernel, n, cap), out_shape=jax.Sha...  47.2 us
    unnamed x5, local copies, waits for them, and re-layouts  2.38 us

profile of v1, /device:TPU:0, one launch (start us, length us, event | category | flops | bytes accessed | tf_op | source)
XLA Modules:
  0.0 49.5 jit_solution(10385792523439588446)
XLA Ops:
  0.0 0.0 copy-start.1
  0.0 0.7 %copy-done.1 = s32[256]{0:T(256)S(1)} copy-done((s32[256]{0:T(256)S(1)}, s32[256]{0:T(256)}, u32[]{:S(2)}) %copy-start.1) | copy-done | bytes 1048
  0.7 0.0 copy-start
  0.7 1.1 %copy-done = f32[256,768]{1,0:T(8,128)S(1)} copy-done((f32[256,768]{1,0:T(8,128)S(1)}, f32[256,768]{1,0:T(8,128)}, u32[]{:S(2)}) %copy-start) | copy-done | bytes 786456
  1.8 47.2 %shard_map.28 = f32[1,256]{1,0:T(1,128)S(1)} custom-call(f32[256,768]{1,0:T(8,128)S(1)} %copy-done, s32[1,256]{1,0:T(1,128)S(1)} %bitcast.3), custom_call_target="tpu_custom_call" | custom-call | tf_op jit(solution)/shard_map/pallas_call | solution.py:212
  49.0 0.6 %copy.4 = f32[256]{0:T(256)} copy(f32[256]{0:T(256)S(1)} %bitcast.2) | data formatting | bytes 2048
Async XLA Ops:
  0.0 0.7 %copy-start.1 = (s32[256]{0:T(256)S(1)}, s32[256]{0:T(256)}, u32[]{:S(2)}) copy-start(s32[256]{0:T(256)} %param.3) | copy-start | bytes 3076
  0.7 1.1 %copy-start = (f32[256,768]{1,0:T(8,128)S(1)}, f32[256,768]{1,0:T(8,128)}, u32[]{:S(2)}) copy-start(f32[256,768]{1,0:T(8,128)} %emb_ref.1) | copy-start | bytes 2359300

commit v2 on v1

--- a/solution.py
+++ b/solution.py
@@ -24,11 +24,17 @@
     return high, low
 
 
+def split3(x):
+    high, rest = split(x)
+    low = x - high.astype(jnp.float32) - rest.astype(jnp.float32)
+    return high, rest, low.astype(jnp.bfloat16)
+
+
 def dedup_kernel(
-    n, cap, emb_ref, clu_ref, out_ref,
-    unit_hi, unit_lo, slot_of, send_rows, got_rows, got_hi, got_lo,
+    n, cap, emb_hbm, clu_hbm, out_ref,
+    emb_ref, clu_ref, unit_hi, unit_lo, slot_of, send_rows, got_rows, got_hi, got_lo,
     send_lab, got_lab, lab_col, best, got_best,
-    row_send, row_recv, lab_send, lab_recv, best_send, best_recv,
+    in_sems, row_send, row_recv, lab_send, lab_recv, best_send, best_recv,
 ):
     rows, width = emb_ref.shape
     per = LANES // cap
@@ -41,15 +47,44 @@
             return lax.bitwise_xor(my_plane, jnp.int32(step))
         return lax.rem(my_plane + step, planes)
 
+    def others(do):
+        for step in range(1, n):
+            do(lax.rem(me + step, n))
+
+    clu_in = pltpu.make_async_copy(clu_hbm, clu_ref, in_sems.at[0])
+    emb_in = pltpu.make_async_copy(emb_hbm, emb_ref, in_sems.at[1])
+    clu_in.start()
+    emb_in.start()
+
     barrier = pltpu.get_barrier_semaphore()
-
-    def greet(step, _):
-        peer = lax.rem(me + step, n)
-        pl.semaphore_signal(barrier, inc=1, device_id={"owners": peer}, device_id_type=MESH)
-        return 0
-
-    lax.fori_loop(1, n, greet, 0)
-
+    others(
+        lambda peer: pl.semaphore_signal(
+            barrier, inc=1, device_id={"owners": peer}, device_id_type=MESH
+        )
+    )
+
+    def remote(src, dst, send, recv, peer):
+        return pltpu.make_async_remote_copy(
+            src_ref=src, dst_ref=dst, send_sem=send, recv_sem=recv,
+            device_id={"owners": peer}, device_id_type=MESH,
+        )
+
+    def label_copy(peer):
+        return remote(send_lab.at[peer], got_lab.at[me], lab_send, lab_recv, peer)
+
+    def row_copy(peer):
+        return remote(
+            send_rows.at[peer], got_rows.at[me], row_send, row_recv.at[my_plane], peer
+        )
+
+    def best_copy(peer):
+        return remote(best.at[peer // per], got_best.at[me], best_send, best_recv, peer)
+
+    def batch(buffer, first, count, send, recv):
+        part = buffer.at[pl.ds(first, count)]
+        return remote(part, part, send, recv, me)
+
+    clu_in.wait()
     clu = clu_ref[...].astype(jnp.float32)
     label = jnp.floor((clu + 0.5) * (1.0 / n))
     dest = clu - label * n
@@ -63,8 +98,8 @@
     ).astype(jnp.bfloat16)
     ranks = jnp.dot(member, earlier, preferred_element_type=jnp.float32)
     slot_of[...] = jnp.where(mine, ranks, -1.0)
+
     rank = jnp.sum(jnp.where(mine, ranks, 0.0), axis=0, keepdims=True)
-
     lane_of = lax.broadcasted_iota(jnp.int32, (LANES, rows), 0).astype(jnp.float32)
     placed_labels = lax.dot_general(
         jnp.where(mine, label, 0.0), (lane_of == rank).astype(jnp.float32), NT,
@@ -73,51 +108,12 @@
     for o in range(n):
         send_lab[o] = placed_labels[o : o + 1]
 
-    unit = to_unit(emb_ref[...])
-    unit_hi[...], unit_lo[...] = split(unit)
-
-    pl.semaphore_wait(barrier, n - 1)
-
-    def label_copy(peer):
-        return pltpu.make_async_remote_copy(
-            src_ref=send_lab.at[peer], dst_ref=got_lab.at[me],
-            send_sem=lab_send.at[peer], recv_sem=lab_recv.at[me],
-            device_id={"owners": peer}, device_id_type=MESH,
-        )
-
-    def row_copy(peer):
-        return pltpu.make_async_remote_copy(
-            src_ref=send_rows.at[peer], dst_ref=got_rows.at[me],
-            send_sem=row_send.at[peer], recv_sem=row_recv.at[me],
-            device_id={"owners": peer}, device_id_type=MESH,
-        )
-
-    def best_copy(peer):
-        return pltpu.make_async_remote_copy(
-            src_ref=best.at[peer // per], dst_ref=got_best.at[me],
-            send_sem=best_send.at[peer], recv_sem=best_recv.at[me],
-            device_id={"owners": peer}, device_id_type=MESH,
-        )
-
-    def arrived(buffer, sems, source):
-        pltpu.make_async_remote_copy(
-            src_ref=buffer.at[source], dst_ref=buffer.at[source],
-            send_sem=sems.at[source], recv_sem=sems.at[source],
-            device_id={"owners": source}, device_id_type=MESH,
-        ).wait_recv()
-
-    def others(do):
-        def step_of(step, _):
-            do(lax.rem(me + step, n))
-            return 0
-
-        lax.fori_loop(1, n, step_of, 0)
-
-    got_lab[me] = send_lab[me]
+    emb_in.wait()
+    unit_hi[...], unit_lo[...] = split(to_unit(emb_ref[...]))
 
     place = lax.broadcasted_iota(jnp.int32, (cap, rows), 0).astype(jnp.float32)
-    order = ORDER if planes == 4 else tuple(range(planes))[::-1]
-    for number, step in enumerate(order):
+
+    def put(step):
         first = plane_at(step) * per
         placing = jnp.concatenate(
             [(place == slot_of[pl.ds(first + i, 1), :]).astype(jnp.float32) for i in range(per)], axis=0
@@ -127,20 +123,31 @@
         )
         for i in range(per):
             send_rows[first + i] = block[i * cap : (i + 1) * cap]
-        for i in range(per):
-            peer = first + i
-            if step == 0:
-                @pl.when(peer != me)
-                def _():
-                    row_copy(peer).start()
-            else:
-                row_copy(peer).start()
-        if number == 0:
-            others(lambda peer: label_copy(peer).start())
-
+
+    def send(step):
+        first = plane_at(step) * per
+        if step == 0:
+            for i in range(1, per):
+                row_copy(first + lax.rem(me - first + i, per)).start()
+        else:
+            for i in range(per):
+                row_copy(first + lax.rem(me + i, per)).start()
+
+    order = ORDER if planes == 4 else tuple(range(planes))[::-1]
+    put(order[0])
+    pl.semaphore_wait(barrier, n - 1)
+    others(lambda peer: label_copy(peer).start())
+    got_lab[me] = send_lab[me]
+    send(order[0])
+    for step in order[1:]:
+        put(step)
+        send(step)
     got_rows[me] = send_rows[me]
 
-    others(lambda peer: arrived(got_lab, lab_recv, peer))
+    offset = (lax.rem(me, per) * cap).astype(jnp.float32)
+    lookup = (lane_of == rank + offset).astype(jnp.bfloat16)
+
+    batch(got_lab, 0, n - 1, lab_send, lab_recv).wait()
     eye = lax.broadcasted_iota(jnp.int32, (cap, LANES), 0) == lax.broadcasted_iota(
         jnp.int32, (cap, LANES), 1
     )
@@ -157,14 +164,8 @@
     lane_at = lax.broadcasted_iota(jnp.int32, square, 1)
     for step in range(planes):
         new = plane_at(step)
-        for i in range(per):
-            source = new * per + i
-            if step == 0:
-                @pl.when(source != me)
-                def _():
-                    arrived(got_rows, row_recv, source)
-            else:
-                arrived(got_rows, row_recv, source)
+        count = per - 1 if step == 0 else per
+        batch(got_rows, 0, count, row_send, row_recv.at[new]).wait_recv()
         block = got_rows[pl.ds(new * per, per)].reshape(LANES, width)
         got_hi[new], got_lo[new] = split(block)
         for past in range(step + 1):
@@ -183,24 +184,17 @@
             top = jnp.max(jnp.where(valid, scores, -1.0), axis=0, keepdims=True)
             best[high] = jnp.maximum(best[high], top)
 
+    others(lambda peer: best_copy(peer).start())
     got_best[me] = best[my_plane]
-    others(lambda peer: best_copy(peer).start())
-    others(lambda peer: arrived(got_best, best_recv, peer))
-
-    offset = (lax.rem(me, per) * cap).astype(jnp.float32)
+    batch(send_rows, 0, n - 1, row_send, row_recv.at[0]).wait_send()
+    batch(got_best, 0, n - 1, best_send, best_recv).wait()
+
     back = jnp.concatenate([got_best[o] for o in range(n)], axis=0)
     spread = jnp.dot(
-        back, (lane_of == rank + offset).astype(jnp.float32),
-        precision=lax.Precision.HIGHEST, preferred_element_type=jnp.float32,
-    )
+        jnp.concatenate(split3(back), axis=0), lookup, preferred_element_type=jnp.float32
+    )
+    spread = spread[:n] + spread[n : 2 * n] + spread[2 * n :]
     out_ref[...] = jnp.sum(jnp.where(mine, spread, 0.0), axis=0, keepdims=True)
-
-    def drain(peer):
-        row_copy(peer).wait_send()
-        label_copy(peer).wait_send()
-        best_copy(peer).wait_send()
-
-    others(drain)
 
 
 def fused(embeddings, cluster_ids):
@@ -212,9 +206,11 @@
     out = pl.pallas_call(
         functools.partial(dedup_kernel, n, cap),
         out_shape=jax.ShapeDtypeStruct((1, rows), f32),
-        in_specs=[pl.BlockSpec(memory_space=pltpu.VMEM)] * 2,
+        in_specs=[pl.BlockSpec(memory_space=pltpu.HBM)] * 2,
         out_specs=pl.BlockSpec(memory_space=pltpu.VMEM),
         scratch_shapes=[
+            pltpu.VMEM((rows, width), f32),
+            pltpu.VMEM((1, rows), jnp.int32),
             pltpu.VMEM((rows, width), bf16),
             pltpu.VMEM((rows, width), bf16),
             pltpu.VMEM((n, rows), f32),
@@ -227,8 +223,8 @@
             pltpu.VMEM((planes, LANES, LANES), f32),
             pltpu.VMEM((planes, 1, LANES), f32),
             pltpu.VMEM((n, 1, LANES), f32),
-        ]
-        + [dma((n,))] * 6,
+            dma((2,)), dma, dma((planes,)), dma, dma, dma, dma,
+        ],
         compiler_params=pltpu.CompilerParams(
             collective_id=0, has_side_effects=True, vmem_limit_bytes=32 * 1024 * 1024
         ),

time: 49.7 us -> 48.4 us (0.974)
  Pallas kernels: 47.2 us -> 45.9 us
    pallas_call x1, Pallas kernels: 47.2 us -> 45.9 us  [fused(): pl.pallas_call(functools.partial(dedup_kernel, n, cap), out_shape=jax.Sha...]
where the time goes in v2:
time: 48.4 us; the launch traced here: 48.2 us
  Pallas kernels  45.9 us (95%)
  local copies, waits for them, and re-layouts  2.38 us (5%)
    pallas_call x1, Pallas kernels, fused(): pl.pallas_call(functools.partial(dedup_kernel, n, cap), out_shape=jax.Sha...  45.9 us
    unnamed x5, local copies, waits for them, and re-layouts  2.38 us

profile of v2, /device:TPU:0, one launch (start us, length us, event | category | flops | bytes accessed | tf_op | source)
XLA Modules:
  0.0 48.2 jit_solution(17988970752490430213)
XLA Ops:
  0.0 0.0 copy-start.1
  0.0 0.7 %copy-done.1 = s32[256]{0:T(256)S(1)} copy-done((s32[256]{0:T(256)S(1)}, s32[256]{0:T(256)}, u32[]{:S(2)}) %copy-start.1) | copy-done | bytes 1048
  0.7 0.0 copy-start
  0.7 1.1 %copy-done = f32[256,768]{1,0:T(8,128)S(1)} copy-done((f32[256,768]{1,0:T(8,128)S(1)}, f32[256,768]{1,0:T(8,128)}, u32[]{:S(2)}) %copy-start) | copy-done | bytes 786456
  1.8 45.9 %shard_map.28 = f32[1,256]{1,0:T(1,128)S(1)} custom-call(f32[256,768]{1,0:T(8,128)S(1)} %copy-done, s32[1,256]{1,0:T(1,128)S(1)} %bitcast.3), custom_call_target="tpu_custom_call" | custom-call | tf_op jit(solution)/shard_map/pallas_call | solution.py:206
  47.7 0.6 %copy.4 = f32[256]{0:T(256)} copy(f32[256]{0:T(256)S(1)} %bitcast.2) | data formatting | bytes 2048
Async XLA Ops:
  0.0 0.7 %copy-start.1 = (s32[256]{0:T(256)S(1)}, s32[256]{0:T(256)}, u32[]{:S(2)}) copy-start(s32[256]{0:T(256)} %param.3) | copy-start | bytes 3076
  0.7 1.1 %copy-start = (f32[256,768]{1,0:T(8,128)S(1)}, f32[256,768]{1,0:T(8,128)}, u32[]{:S(2)}) copy-start(f32[256,768]{1,0:T(8,128)} %emb_hbm.1) | copy-start | bytes 2359300

commit v3 on v2

--- a/solution.py
+++ b/solution.py
@@ -226,7 +226,7 @@
             dma((2,)), dma, dma((planes,)), dma, dma, dma, dma,
         ],
         compiler_params=pltpu.CompilerParams(
-            collective_id=0, has_side_effects=True, vmem_limit_bytes=32 * 1024 * 1024
+            collective_id=0, has_side_effects=True, vmem_limit_bytes=60 * 1024 * 1024
         ),
     )(embeddings, cluster_ids.reshape(1, rows))
     return out.reshape(rows)

time: 48.4 us -> 47.7 us (0.986)
  local copies, waits for them, and re-layouts: 2.38 us -> 1.22 us
    unnamed x5 -> x3, local copies, waits for them, and re-layouts: 2.38 us -> 1.22 us
where the time goes in v3:
time: 47.7 us; the launch traced here: 47.5 us
  Pallas kernels  46.3 us (97%)
  local copies, waits for them, and re-layouts  1.22 us (3%)
    pallas_call x1, Pallas kernels, fused(): pl.pallas_call(functools.partial(dedup_kernel, n, cap), out_shape=jax.Sha...  46.3 us
    unnamed x3, local copies, waits for them, and re-layouts  1.22 us

profile of v3, /device:TPU:0, one launch (start us, length us, event | category | flops | bytes accessed | tf_op | source)
XLA Modules:
  0.0 47.5 jit_solution(2126872488771177542)
XLA Ops:
  0.0 46.3 %shard_map.28 = f32[1,256]{1,0:T(1,128)} custom-call(f32[256,768]{1,0:T(8,128)} %emb_hbm.1, s32[1,256]{1,0:T(1,128)} %bitcast.3), custom_call_target="tpu_custom_call" | custom-call | tf_op jit(solution)/shard_map/pallas_call | solution.py:206
  46.3 0.0 copy-start
  46.3 0.7 %copy-done = f32[1,256]{1,0:T(1,128)S(1)} copy-done((f32[1,256]{1,0:T(1,128)S(1)}, f32[1,256]{1,0:T(1,128)}, u32[]{:S(2)}) %copy-start) | copy-done | bytes 1048
  47.0 0.6 %copy.4 = f32[256]{0:T(256)} copy(f32[256]{0:T(256)S(1)} %bitcast.2) | data formatting | bytes 2048
Async XLA Ops:
  46.3 0.7 %copy-start = (f32[1,256]{1,0:T(1,128)S(1)}, f32[1,256]{1,0:T(1,128)}, u32[]{:S(2)}) copy-start(f32[1,256]{1,0:T(1,128)} %shard_map.28) | copy-start | bytes 3076

commit v4 on v3

--- a/solution.py
+++ b/solution.py
@@ -226,7 +226,7 @@
             dma((2,)), dma, dma((planes,)), dma, dma, dma, dma,
         ],
         compiler_params=pltpu.CompilerParams(
-            collective_id=0, has_side_effects=True, vmem_limit_bytes=60 * 1024 * 1024
+            collective_id=0, has_side_effects=True, vmem_limit_bytes=54784 * 1024
         ),
     )(embeddings, cluster_ids.reshape(1, rows))
     return out.reshape(rows)

time: 47.7 us -> 47.2 us (0.990)
  Pallas kernels: 46.3 us -> 45.7 us
    pallas_call x1, Pallas kernels: 46.3 us -> 45.7 us  [fused(): pl.pallas_call(functools.partial(dedup_kernel, n, cap), out_shape=jax.Sha...]
where the time goes in v4:
time: 47.2 us; the launch traced here: 47 us
  Pallas kernels  45.7 us (97%)
  local copies, waits for them, and re-layouts  1.24 us (3%)
    pallas_call x1, Pallas kernels, fused(): pl.pallas_call(functools.partial(dedup_kernel, n, cap), out_shape=jax.Sha...  45.7 us
    unnamed x3, local copies, waits for them, and re-layouts  1.24 us

profile of v4, /device:TPU:0, one launch (start us, length us, event | category | flops | bytes accessed | tf_op | source)
XLA Modules:
  0.0 47.0 jit_solution(5572115884826511071)
XLA Ops:
  0.0 0.0 copy-start
  0.0 0.7 %copy-done = s32[256]{0:T(256)S(1)} copy-done((s32[256]{0:T(256)S(1)}, s32[256]{0:T(256)}, u32[]{:S(2)}) %copy-start) | copy-done | bytes 1048
  0.7 45.7 %shard_map.28 = f32[1,256]{1,0:T(1,128)S(1)} custom-call(f32[256,768]{1,0:T(8,128)} %emb_hbm.1, s32[1,256]{1,0:T(1,128)S(1)} %bitcast.3), custom_call_target="tpu_custom_call" | custom-call | tf_op jit(solution)/shard_map/pallas_call | solution.py:206
  46.4 0.6 %copy.4 = f32[256]{0:T(256)} copy(f32[256]{0:T(256)S(1)} %bitcast.2) | data formatting | bytes 2048
Async XLA Ops:
  0.0 0.7 %copy-start = (s32[256]{0:T(256)S(1)}, s32[256]{0:T(256)}, u32[]{:S(2)}) copy-start(s32[256]{0:T(256)} %param.3) | copy-start | bytes 3076

commit v5 on v4

--- a/solution.py
+++ b/solution.py
@@ -53,15 +53,15 @@
 
     clu_in = pltpu.make_async_copy(clu_hbm, clu_ref, in_sems.at[0])
     emb_in = pltpu.make_async_copy(emb_hbm, emb_ref, in_sems.at[1])
-    clu_in.start()
-    emb_in.start()
-
     barrier = pltpu.get_barrier_semaphore()
     others(
         lambda peer: pl.semaphore_signal(
             barrier, inc=1, device_id={"owners": peer}, device_id_type=MESH
         )
     )
+
+    clu_in.start()
+    emb_in.start()
 
     def remote(src, dst, send, recv, peer):
         return pltpu.make_async_remote_copy(
@@ -113,8 +113,16 @@
 
     place = lax.broadcasted_iota(jnp.int32, (cap, rows), 0).astype(jnp.float32)
 
+    def target(step):
+        if planes != 4 or step < 2:
+            return plane_at(step)
+        below = my_plane < 2
+        if step == 2:
+            return jnp.where(below, 3, 0)
+        return jnp.where(below, 2, 1)
+
     def put(step):
-        first = plane_at(step) * per
+        first = target(step) * per
         placing = jnp.concatenate(
             [(place == slot_of[pl.ds(first + i, 1), :]).astype(jnp.float32) for i in range(per)], axis=0
         ).astype(jnp.bfloat16)
@@ -125,7 +133,7 @@
             send_rows[first + i] = block[i * cap : (i + 1) * cap]
 
     def send(step):
-        first = plane_at(step) * per
+        first = target(step) * per
         if step == 0:
             for i in range(1, per):
                 row_copy(first + lax.rem(me - first + i, per)).start()
@@ -158,6 +166,19 @@
             )
             lab_col[plane, pl.ds(i * cap, cap), :] = jnp.broadcast_to(column, (cap, LANES))
         best[plane] = jnp.full((1, LANES), -1.0, jnp.float32)
+
+    def give_back(plane):
+        first = plane * per
+
+        @pl.when(plane == my_plane)
+        def _():
+            for i in range(1, per):
+                best_copy(first + lax.rem(me - first + i, per)).start()
+
+        @pl.when(plane != my_plane)
+        def _():
+            for i in range(per):
+                best_copy(first + i).start()
 
     square = (LANES, LANES)
     row_at = lax.broadcasted_iota(jnp.int32, square, 0)
@@ -183,8 +204,22 @@
                 valid = valid & (row_at < lane_at)
             top = jnp.max(jnp.where(valid, scores, -1.0), axis=0, keepdims=True)
             best[high] = jnp.maximum(best[high], top)
-
-    others(lambda peer: best_copy(peer).start())
+        if planes == 4 and step == 1:
+            @pl.when(my_plane < 2)
+            def _():
+                give_back(0)
+                give_back(1)
+
+    if planes == 4:
+        @pl.when(my_plane >= 2)
+        def _():
+            give_back(0)
+            give_back(1)
+
+        give_back(3)
+        give_back(2)
+    else:
+        others(lambda peer: best_copy(peer).start())
     got_best[me] = best[my_plane]
     batch(send_rows, 0, n - 1, row_send, row_recv.at[0]).wait_send()
     batch(got_best, 0, n - 1, best_send, best_recv).wait()

time: 47.2 us -> 47.2 us (level)
  no operation moved by 1% of the time
where the time goes in v5:
time: 47.2 us; the launch traced here: 47 us
  Pallas kernels  45.7 us (97%)
  local copies, waits for them, and re-layouts  1.24 us (3%)
    pallas_call x1, Pallas kernels, fused(): pl.pallas_call(functools.partial(dedup_kernel, n, cap), out_shape=jax.Sha...  45.7 us
    unnamed x3, local copies, waits for them, and re-layouts  1.24 us

profile of v5, /device:TPU:0, one launch (start us, length us, event | category | flops | bytes accessed | tf_op | source)
XLA Modules:
  0.0 47.0 jit_solution(1670590027066056933)
XLA Ops:
  0.0 0.0 copy-start
  0.0 0.7 %copy-done = s32[256]{0:T(256)S(1)} copy-done((s32[256]{0:T(256)S(1)}, s32[256]{0:T(256)}, u32[]{:S(2)}) %copy-start) | copy-done | bytes 1048
  0.7 45.7 %shard_map.28 = f32[1,256]{1,0:T(1,128)S(1)} custom-call(f32[256,768]{1,0:T(8,128)} %emb_hbm.1, s32[1,256]{1,0:T(1,128)S(1)} %bitcast.3), custom_call_target="tpu_custom_call" | custom-call | tf_op jit(solution)/shard_map/pallas_call | solution.py:241
  46.4 0.6 %copy.4 = f32[256]{0:T(256)} copy(f32[256]{0:T(256)S(1)} %bitcast.2) | data formatting | bytes 2048
Async XLA Ops:
  0.0 0.7 %copy-start = (s32[256]{0:T(256)S(1)}, s32[256]{0:T(256)}, u32[]{:S(2)}) copy-start(s32[256]{0:T(256)} %param.3) | copy-start | bytes 3076
